TPU v7x, 256 devices: a whole 4x4x8 slice. The times are simulated.
256 devices in a mesh: chan: 32 (over x, y, core), tm: 8 (over z).
Axes of the slice: x: 4, y: 4, z: 8, core: 2. Of those that a mesh axis runs over, the one named last changes fastest.
Arguments:
- visibilities: bfloat16 [384, 2, 6144, 128], P('chan', None, 'tm'), may hold values from -6 to 6
- vis_weight: bfloat16 [6144, 128], P('tm'), may hold values from 0.19921875 to 2
- tile_index: int32 [6144], P('tm'), may hold values from 0 to 255
- tile_offset: int32 [6144, 128], P('tm'), may hold values from 0 to 255
- live_count: int32 [8, 768], P('tm'), may hold values from 1 to 128, 49152 in all within a row
Outputs:
- spectra: float32 [2, 384, 65536], P(None, None, ('tm', 'chan'))
Inputs may be any that keep to these rules, and one draw needn't show every extreme that they name: `live_count`: in each time span the counts sum to 49152, and some group holds all 128 slots.
All inputs are finite; a program needn't handle non-finite values.
Results may differ from a plain program's by a relative error of at most 0.0033.
Values sent between devices are 32-bit elements; how exact they have to be, the bound alone decides.
A program may use at most 64 MiB of HBM per device.

v0:
```python
import functools
import math

import jax
import jax.numpy as jnp
import ml_dtypes
import numpy as np
from jax import lax
from jax.experimental import pallas as pl
from jax.experimental.pallas import tpu as pltpu
from jax.sharding import PartitionSpec as P

TSIDE = 16
TILE = TSIDE * TSIDE
LANES = 128
KERNEL_SIGMA2 = 1.44
KERNEL_REACH = 3
HALVES = 2
MESH = pl.DeviceIdType.MESH


def split_bf16(table):
    high = table.astype(ml_dtypes.bfloat16)
    low = (table - high.astype(np.float64)).astype(ml_dtypes.bfloat16)
    return np.stack([high, low])


def spread_table():
    step = np.arange(TSIDE)[:, None] - np.arange(TSIDE)[None, :]
    line = np.where(np.abs(step) <= KERNEL_REACH, np.exp(-step * step / (2.0 * KERNEL_SIGMA2)), 0.0)
    return np.kron(line, line)


def delay_table(channels):
    freq = np.arange(channels)
    angle = 2.0 * np.pi * (freq[:, None] * freq[None, :] % channels) / channels
    phase = 2.0 * np.pi * freq / (channels - 1)
    taper = 0.42323 - 0.49755 * np.cos(phase) + 0.07922 * np.cos(2.0 * phase)
    cos_part = np.cos(angle) * taper[None, :]
    sin_part = np.sin(angle) * taper[None, :]
    upper = np.stack([cos_part, sin_part], axis=-1)
    lower = np.stack([-sin_part, cos_part], axis=-1)
    return np.stack([upper, lower], axis=0).reshape(2 * channels, 2 * channels)


def grid_kernel(tile_ref, live_ref, vis_ref, weight_ref, offset_ref, grid_ref, wgrid_ref):
    step = pl.program_id(0)
    rows, block = vis_ref.shape[0], vis_ref.shape[1]

    @pl.when(step == 0)
    def _():
        grid_ref[...] = jnp.zeros_like(grid_ref)
        wgrid_ref[...] = jnp.zeros_like(wgrid_ref)

    cell = lax.broadcasted_iota(jnp.int32, (LANES, LANES), 0).astype(jnp.int16)
    lane = lax.broadcasted_iota(jnp.int32, (8, LANES), 1)
    half = lax.broadcasted_iota(jnp.int32, (8, LANES), 0)
    zero = jnp.zeros((16, LANES), jnp.bfloat16)

    def some(index, _):
        first = pl.multiple_of(index * 16, 16)
        data = jnp.swapaxes(vis_ref[:, pl.ds(first, 16), :].astype(jnp.float32), 0, 1)
        weights = weight_ref[pl.ds(first, 16), :].astype(jnp.float32)
        for j in range(16):
            group = step * block + first + j
            weight = jnp.where(lane < live_ref[group], jnp.broadcast_to(weights[j:j + 1], (8, LANES)), 0.0)
            offset = jnp.broadcast_to(offset_ref[pl.ds(first + j, 1), :], (8, LANES))
            low = jnp.bitwise_and(offset, LANES - 1)
            high = jnp.right_shift(offset, 7)
            low16 = jnp.concatenate([low, low], 0).astype(jnp.int16)
            weight16 = jnp.concatenate([weight, weight], 0).astype(jnp.bfloat16)
            hot = jnp.concatenate(
                [jnp.where(cell[16 * k:16 * k + 16] == low16, weight16, zero) for k in range(8)], 0
            )
            parts = [
                jnp.where(high == a, data[j, 8 * q:8 * q + 8], 0.0)
                for a in range(HALVES)
                for q in range(rows // 8)
            ]
            parts.append(jnp.where(high == half, 1.0, 0.0))
            left = jnp.concatenate(parts, 0).astype(jnp.bfloat16)
            total = lax.dot_general(left, hot, (((1,), (1,)), ((), ())), preferred_element_type=jnp.float32)
            tile = tile_ref[group]
            grid_ref[tile] += total[:HALVES * rows]
            wgrid_ref[tile] += total[HALVES * rows:]
        return 0

    lax.fori_loop(0, block // 16, some, 0, unroll=True)


def gridding(data, weight, tiles, offset, live, n_tile):
    rows, groups, slots = data.shape
    block = math.gcd(groups, 64)
    return pl.pallas_call(
        grid_kernel,
        grid_spec=pltpu.PrefetchScalarGridSpec(
            num_scalar_prefetch=2,
            grid=(groups // block,),
            in_specs=[
                pl.BlockSpec((rows, block, slots), lambda i, *_: (0, i, 0)),
                pl.BlockSpec((block, slots), lambda i, *_: (i, 0)),
                pl.BlockSpec((block, slots), lambda i, *_: (i, 0)),
            ],
            out_specs=[
                pl.BlockSpec((n_tile, HALVES * rows, LANES), lambda i, *_: (0, 0, 0), pipeline_mode=pl.Buffered(1)),
                pl.BlockSpec((n_tile, 8, LANES), lambda i, *_: (0, 0, 0), pipeline_mode=pl.Buffered(1)),
            ],
        ),
        out_shape=[
            jax.ShapeDtypeStruct((n_tile, HALVES * rows, LANES), jnp.float32),
            jax.ShapeDtypeStruct((n_tile, 8, LANES), jnp.float32),
        ],
        compiler_params=pltpu.CompilerParams(vmem_limit_bytes=20 << 20),
        cost_estimate=pl.CostEstimate(flops=2 * groups * rows * slots * TILE, bytes_accessed=data.size * 2, transcendentals=0),
        name="gridding",
    )(tiles, live, data, weight, offset)


def dot3(left, right):
    dot = functools.partial(jnp.dot, preferred_element_type=jnp.float32)
    return dot(left[0], right[0]) + (dot(left[0], right[1]) + dot(left[1], right[0]))


def pair(x):
    high = x.astype(jnp.bfloat16)
    return high, (x - high.astype(jnp.float32)).astype(jnp.bfloat16)


def exchange_kernel(
    n_time, n_chan, per, grid_ref, wgrid_ref, delay_hbm, spread_hbm, out_ref,
    ring, mine, gathered, wparts, delay, spread,
    ring_send, ring_recv, plane_send, plane_recv, w_send, w_recv, table_sem,
):
    me_t = lax.axis_index("tm")
    me_c = lax.axis_index("chan")
    pieces = n_chan // per
    reach = n_time // 2
    rows2 = grid_ref.shape[1]
    rows = rows2 // HALVES
    turn = me_c // per
    neighbour = (lax.rem(me_t + 1, n_time), lax.rem(me_t + n_time - 1, n_time))

    tables = [pltpu.make_async_copy(delay_hbm, delay, table_sem.at[0]),
              pltpu.make_async_copy(spread_hbm, spread, table_sem.at[1])]
    for copy in tables:
        copy.start()

    barrier = pltpu.get_barrier_semaphore()

    def greet_t(k, _):
        pl.semaphore_signal(barrier, inc=1, device_id={"tm": lax.rem(me_t + k, n_time)}, device_id_type=MESH)
        return 0

    def greet_c(k, _):
        pl.semaphore_signal(barrier, inc=1, device_id={"chan": lax.rem(me_c + k, n_chan)}, device_id_type=MESH)
        return 0

    lax.fori_loop(1, n_time, greet_t, 0)
    lax.fori_loop(1, n_chan, greet_c, 0)
    pl.semaphore_wait(barrier, n_time - 1 + n_chan - 1)

    def span(slot):
        return pl.ds(lax.rem(slot + turn, pieces) * per, per)

    def grid_span(chunk, slot):
        return pl.ds(chunk * n_chan + lax.rem(slot + turn, pieces) * per, per)

    def chunk_of(way, step):
        away = reach - step
        return lax.rem(me_t + (away if way == 0 else n_time - away), n_time)

    def ring_copy(way, step, slot, raw):
        source = grid_ref.at[grid_span(chunk_of(way, step), slot)] if raw else ring.at[way, step - 1, span(slot)]
        return pltpu.make_async_remote_copy(
            src_ref=source,
            dst_ref=ring.at[way, step, span(slot)],
            send_sem=ring_send.at[way, step, slot],
            recv_sem=ring_recv.at[way, step, slot],
            device_id={"tm": neighbour[way]},
            device_id_type=MESH,
        )

    half = pieces // 2

    def open_ring(slot, _):
        ring_copy(0, 0, slot, True).start()
        ring_copy(1, 0, slot + half, True).start()
        return 0

    lax.fori_loop(0, half, open_ring, 0)

    def w_copy(k):
        other = lax.rem(me_t + k, n_time)
        return pltpu.make_async_remote_copy(
            src_ref=wgrid_ref.at[other * n_chan + me_c],
            dst_ref=wparts.at[k],
            send_sem=w_send.at[k],
            recv_sem=w_recv.at[k],
            device_id={"tm": other},
            device_id_type=MESH,
        )

    lax.fori_loop(1, n_time, lambda k, _: (w_copy(k).start(), 0)[1], 0)

    def hop(step, fresh):
        def body(slot, _):
            for way in range(2):
                if fresh[way]:
                    ring_copy(way, step, slot, True).start()
                else:
                    ring_copy(way, step - 1, slot, True).wait_recv()
                    ring[way, step - 1, span(slot)] += grid_ref[grid_span(chunk_of(way, step), slot)]
                    ring_copy(way, step, slot, False).start()
            return 0
        return body

    lax.fori_loop(0, half, hop(1, (False, True)), 0)
    lax.fori_loop(half, pieces, hop(1, (True, False)), 0)
    for step in range(2, reach):
        lax.fori_loop(0, pieces, hop(step, (False, False)), 0)

    def plane_copy(other):
        return pltpu.make_async_remote_copy(
            src_ref=mine.at[other],
            dst_ref=gathered.at[me_c],
            send_sem=plane_send.at[other],
            recv_sem=plane_recv.at[me_c],
            device_id={"chan": other},
            device_id_type=MESH,
        )

    def finish(slot, _):
        for way in range(2):
            ring_copy(way, reach - 1, slot, True).wait_recv()
        where = span(slot)
        mine[where] = grid_ref[grid_span(me_t, slot)] + ring[0, reach - 1, where] + ring[1, reach - 1, where]
        for q in range(per):
            other = lax.rem(slot + turn, pieces) * per + q

            @pl.when(other != me_c)
            def _():
                plane_copy(other).start()

            @pl.when(other == me_c)
            def _():
                gathered[me_c] = mine[me_c]
        return 0

    lax.fori_loop(0, pieces, finish, 0)

    def w_wait(k, _):
        w_copy(k).wait_recv()
        return 0

    lax.fori_loop(1, n_time, w_wait, 0)
    wsum = wgrid_ref[me_t * n_chan + me_c]
    for k in range(1, n_time):
        wsum = wsum + wparts[k]
    for copy in tables:
        copy.wait()
    wcells = jnp.concatenate([jnp.broadcast_to(wsum[a:a + 1], (8, LANES)) for a in range(HALVES)], 1)
    spread_pair = (spread[0], spread[1])
    scale = 1.0 / jnp.maximum(dot3(pair(wcells), spread_pair)[0:1], 1.0)

    def plane_wait(k, _):
        other = lax.rem(me_c + k, n_chan)
        pltpu.make_async_remote_copy(
            src_ref=mine.at[other],
            dst_ref=gathered.at[other],
            send_sem=plane_send.at[other],
            recv_sem=plane_recv.at[other],
            device_id={"chan": other},
            device_id_type=MESH,
        ).wait_recv()
        return 0

    lax.fori_loop(1, n_chan, plane_wait, 0)
    cells = jnp.concatenate(
        [gathered[:, a * rows:(a + 1) * rows, :].reshape(n_chan * rows, LANES) for a in range(HALVES)], 1
    )
    normal = pair(dot3(pair(cells), spread_pair) * scale)
    out_ref[...] = dot3((delay[0], delay[1]), normal)

    def drain_ring(way, step, low, high):
        lax.fori_loop(low, high, lambda slot, _: (ring_copy(way, step, slot, True).wait_send(), 0)[1], 0)

    drain_ring(0, 0, 0, half)
    drain_ring(1, 0, half, pieces)
    for step in range(1, reach):
        for way in range(2):
            drain_ring(way, step, 0, pieces)
    lax.fori_loop(1, n_time, lambda k, _: (w_copy(k).wait_send(), 0)[1], 0)
    lax.fori_loop(1, n_chan, lambda k, _: (plane_copy(lax.rem(me_c + k, n_chan)).wait_send(), 0)[1], 0)


def exchange(grid, wgrid, n_time, n_chan):
    rows2 = grid.shape[1]
    rows = rows2 // HALVES
    total = rows * n_chan
    per = max(1, n_chan // 8)
    pieces = n_chan // per
    reach = n_time // 2
    delay = jnp.asarray(split_bf16(delay_table(total // 2)))
    spread = jnp.asarray(split_bf16(spread_table()))
    vmem = pl.BlockSpec(memory_space=pltpu.VMEM)
    hbm = pl.BlockSpec(memory_space=pl.ANY)
    return pl.pallas_call(
        functools.partial(exchange_kernel, n_time, n_chan, per),
        in_specs=[vmem, vmem, hbm, hbm],
        out_specs=vmem,
        out_shape=jax.ShapeDtypeStruct((total, TILE), jnp.float32),
        scratch_shapes=[
            pltpu.VMEM((2, reach, n_chan, rows2, LANES), jnp.float32),
            pltpu.VMEM((n_chan, rows2, LANES), jnp.float32),
            pltpu.VMEM((n_chan, rows2, LANES), jnp.float32),
            pltpu.VMEM((n_time, 8, LANES), jnp.float32),
            pltpu.VMEM(delay.shape, jnp.bfloat16),
            pltpu.VMEM(spread.shape, jnp.bfloat16),
            pltpu.SemaphoreType.DMA((2, reach, pieces)),
            pltpu.SemaphoreType.DMA((2, reach, pieces)),
            pltpu.SemaphoreType.DMA((n_chan,)),
            pltpu.SemaphoreType.DMA((n_chan,)),
            pltpu.SemaphoreType.DMA((n_time,)),
            pltpu.SemaphoreType.DMA((n_time,)),
            pltpu.SemaphoreType.DMA((2,)),
        ],
        compiler_params=pltpu.CompilerParams(collective_id=0, has_side_effects=True, vmem_limit_bytes=40 << 20),
        name="exchange",
    )(grid, wgrid, delay, spread)


def local(visibilities, vis_weight, tile_index, tile_offset, live_count):
    channels, parts, groups, slots = visibilities.shape
    n_chan = lax.axis_size("chan")
    n_time = lax.axis_size("tm")
    data = visibilities.reshape(channels * parts, groups, slots)
    grid, wgrid = gridding(data, vis_weight, tile_index, tile_offset, live_count.reshape(groups), n_chan * n_time)
    result = exchange(grid, wgrid, n_time, n_chan)
    return result.reshape(2, channels * n_chan, TILE)


def solution(mesh):
    placed = (P("chan", None, "tm", None), P("tm", None), P("tm"), P("tm", None), P("tm", None))
    return jax.shard_map(
        local, mesh=mesh, in_specs=placed, out_specs=P(None, None, ("tm", "chan")), check_vma=False
    )
```

profile of v0, /device:TPU:1, one launch (start us, length us, event | category | flops | bytes accessed | tf_op | source)
XLA Modules:
  0.0 108.9 jit_solution(12509028519450230346)
XLA Ops:
  0.0 0.7 reduce.live_ref
  0.7 0.0 copy-start
  0.7 2.3 %copy-done = bf16[12,2,768,128]{3,2,1,0:T(8,128)(2,1)S(1)} copy-done((bf16[12,2,768,128]{3,2,1,0:T(8,128)(2,1)S(1)}, bf16[12,2,768,128]{3,2,1,0:T(8,128)(2,1)}, u32[]{:S(2)}) %copy-start) | copy-done | bytes 4718616
  3.0 0.0 copy-start.2
  3.0 1.0 copy-done.2
  4.0 0.0 copy-start.4
  4.0 0.9 copy-done.4
  5.0 0.0 copy-start.5
  5.0 0.7 copy-done.5
  5.7 0.0 copy-start.1
  5.7 0.0 copy-start.3
  5.7 20.1 %gridding.1 = (f32[256,48,128]{2,1,0:T(8,128)S(1)}, f32[256,8,128]{2,1,0:T(8,128)S(1)}) custom-call(s32[768]{0:T(1024)S(1)} %copy-done.5, s32[768]{0:T(1024)S(1)} %reduce.live_ref, bf16[24,768,128]{2,1,0:T(8,128)(2,1)S(1)} %bitcast.2, bf16[768,128]{1,0:T(8,128)(2,1)S(1)} %copy-done.4, s32[768,128]{1,0:T(8,128)S(1)} %copy-done.2), custom_call_target="tpu_custom_call" | custom-call | flops 1207959552 | bytes 4718592 | tf_op jit(solution)/shard_map/gridding/pallas_call | solution.py:94
  25.8 0.0 copy-done.1
  25.8 0.0 copy-done.3
  25.8 82.2 %exchange.1 = f32[768,256]{1,0:T(8,128)S(1)} custom-call(f32[256,48,128]{2,1,0:T(8,128)S(1)} %get-tuple-element.7.grid_ref, f32[256,8,128]{2,1,0:T(8,128)S(1)} %get-tuple-element.8.wgrid_ref, bf16[2,768,768]{2,1,0:T(8,128)(2,1)S(1)} %copy-done.1, bf16[2,256,256]{2,1,0:T(8,128)(2,1)S(1)} %copy-done.3), custom_call_target="tpu_custom_call" | custom-call | tf_op jit(solution)/shard_map/exchange/pallas_call | solution.py:307
  108.1 0.9 copy.9
Async XLA Ops:
  0.7 2.3 %copy-start = (bf16[12,2,768,128]{3,2,1,0:T(8,128)(2,1)S(1)}, bf16[12,2,768,128]{3,2,1,0:T(8,128)(2,1)}, u32[]{:S(2)}) copy-start(bf16[12,2,768,128]{3,2,1,0:T(8,128)(2,1)} %param.7) | copy-start | bytes 14155780
  3.0 1.0 copy-start.2
  4.0 0.9 copy-start.4
  5.0 0.7 copy-start.5
  5.7 20.2 %copy-start.1 = (bf16[2,768,768]{2,1,0:T(8,128)(2,1)S(1)}, bf16[2,768,768]{2,1,0:T(8,128)(2,1)}, u32[]{:S(2)}) copy-start(bf16[2,768,768]{2,1,0:T(8,128)(2,1)} %constant.4.clone.delay_hbm) | copy-start | bytes 7077892
  5.7 20.2 %copy-start.3 = (bf16[2,256,256]{2,1,0:T(8,128)(2,1)S(1)}, bf16[2,256,256]{2,1,0:T(8,128)(2,1)}, u32[]{:S(2)}) copy-start(bf16[2,256,256]{2,1,0:T(8,128)(2,1)} %constant.5.clone.spread_hbm) | copy-start | bytes 786436
where the time goes:
time: 109 us
  Pallas kernels  102 us (94%)
  local copies, waits for them, and re-layouts  5.83 us (5%)
    pallas_call x1, Pallas kernels, exchange(): pl.pallas_call(functools.partial(exchange_kernel, n_time, n_chan, per), i...  82.2 us
    pallas_call x1, Pallas kernels, gridding(): pl.pallas_call(grid_kernel, grid_spec=pltpu.PrefetchScalarGridSpec(num_sc...  20.1 us
    unnamed x13, local copies, waits for them, and re-layouts  5.83 us

commit v1 on v0

--- a/solution.py
+++ b/solution.py
@@ -43,77 +43,159 @@
     return np.stack([upper, lower], axis=0).reshape(2 * channels, 2 * channels)
 
 
-def grid_kernel(tile_ref, live_ref, vis_ref, weight_ref, offset_ref, grid_ref, wgrid_ref):
-    step = pl.program_id(0)
-    rows, block = vis_ref.shape[0], vis_ref.shape[1]
-
-    @pl.when(step == 0)
-    def _():
-        grid_ref[...] = jnp.zeros_like(grid_ref)
-        wgrid_ref[...] = jnp.zeros_like(wgrid_ref)
+def in_hbm(x):
+    return pltpu.with_memory_space_constraint(x, pltpu.HBM)
+
+
+BATCH = 16
+PUSH = 4
+
+
+def chunks_of(groups):
+    cuts = [32, 96, 128]
+    if groups < 2 * sum(cuts):
+        return [groups]
+    rest = groups - sum(cuts)
+    return cuts + [rest // 2, rest - rest // 2]
+
+
+def grid_kernel(
+    live_hbm, tile_hbm, vis_hbm, weight_hbm, offset_hbm, grid_ref, wgrid_ref,
+    live_ref, tile_ref, vis_ref, weight_ref, offset_ref, vis_sem, small_sem,
+):
+    rows, groups = vis_ref.shape[:2]
+    cuts = chunks_of(groups)
+    starts = [sum(cuts[:n]) for n in range(len(cuts))]
+
+    def vis_copy(n):
+        part = pl.ds(starts[n], cuts[n])
+        return pltpu.make_async_copy(vis_hbm.at[:, part], vis_ref.at[:, part], vis_sem.at[n])
+
+    pairs = [(weight_hbm, weight_ref), (offset_hbm, offset_ref), (live_hbm, live_ref), (tile_hbm, tile_ref)]
+    small = [pltpu.make_async_copy(a, b, small_sem.at[n]) for n, (a, b) in enumerate(pairs)]
+    vis_copy(0).start()
+    for copy in small:
+        copy.start()
+    for n in range(1, len(cuts)):
+        vis_copy(n).start()
+
+    @pl.loop(0, grid_ref.shape[0] // 8)
+    def _(i):
+        some = pl.ds(i * 8, 8)
+        grid_ref[some] = jnp.zeros((8, *grid_ref.shape[1:]), jnp.float32)
+        wgrid_ref[some] = jnp.zeros((8, *wgrid_ref.shape[1:]), jnp.float32)
+
+    for copy in small:
+        copy.wait()
 
     cell = lax.broadcasted_iota(jnp.int32, (LANES, LANES), 0).astype(jnp.int16)
     lane = lax.broadcasted_iota(jnp.int32, (8, LANES), 1)
-    half = lax.broadcasted_iota(jnp.int32, (8, LANES), 0)
+    sub = lax.broadcasted_iota(jnp.int32, (8, LANES), 0)
     zero = jnp.zeros((16, LANES), jnp.bfloat16)
-
-    def some(index, _):
-        first = pl.multiple_of(index * 16, 16)
-        data = jnp.swapaxes(vis_ref[:, pl.ds(first, 16), :].astype(jnp.float32), 0, 1)
-        weights = weight_ref[pl.ds(first, 16), :].astype(jnp.float32)
-        for j in range(16):
-            group = step * block + first + j
-            weight = jnp.where(lane < live_ref[group], jnp.broadcast_to(weights[j:j + 1], (8, LANES)), 0.0)
-            offset = jnp.broadcast_to(offset_ref[pl.ds(first + j, 1), :], (8, LANES))
-            low = jnp.bitwise_and(offset, LANES - 1)
-            high = jnp.right_shift(offset, 7)
-            low16 = jnp.concatenate([low, low], 0).astype(jnp.int16)
-            weight16 = jnp.concatenate([weight, weight], 0).astype(jnp.bfloat16)
-            hot = jnp.concatenate(
-                [jnp.where(cell[16 * k:16 * k + 16] == low16, weight16, zero) for k in range(8)], 0
-            )
-            parts = [
-                jnp.where(high == a, data[j, 8 * q:8 * q + 8], 0.0)
-                for a in range(HALVES)
-                for q in range(rows // 8)
-            ]
-            parts.append(jnp.where(high == half, 1.0, 0.0))
-            left = jnp.concatenate(parts, 0).astype(jnp.bfloat16)
-            total = lax.dot_general(left, hot, (((1,), (1,)), ((), ())), preferred_element_type=jnp.float32)
-            tile = tile_ref[group]
-            grid_ref[tile] += total[:HALVES * rows]
-            wgrid_ref[tile] += total[HALVES * rows:]
-        return 0
-
-    lax.fori_loop(0, block // 16, some, 0, unroll=True)
+    blank = jnp.zeros((HALVES * rows, LANES), jnp.bfloat16)
+
+    def load(first):
+        data = jnp.swapaxes(vis_ref[:, pl.ds(first, BATCH), :].astype(jnp.float32), 0, 1)
+        return data, weight_ref[pl.ds(first, BATCH), :].astype(jnp.float32)
+
+    def inner(*acc):
+        sums, wsums = acc[:BATCH], acc[BATCH:]
+
+        def feed(first, k, data, weights):
+            hots, lefts, highs = [], [], []
+            for i in range(PUSH):
+                j = PUSH * k + i
+                weight = jnp.where(lane < live_ref[0, first + j], jnp.broadcast_to(weights[j:j + 1], (8, LANES)), 0.0)
+                offset = jnp.broadcast_to(offset_ref[pl.ds(first + j, 1), :], (8, LANES))
+                low = jnp.bitwise_and(offset, LANES - 1)
+                high = jnp.right_shift(offset, 7)
+                low16 = jnp.concatenate([low, low], 0).astype(jnp.int16)
+                weight16 = jnp.concatenate([weight, weight], 0).astype(jnp.bfloat16)
+                hots.append(jnp.concatenate(
+                    [jnp.where(cell[16 * q:16 * q + 16] == low16, weight16, zero) for q in range(LANES // 16)], 0
+                ))
+                highs.append(high)
+                parts = [
+                    jnp.where(high == a, data[j, 8 * q:8 * q + 8], 0.0) for a in range(HALVES) for q in range(rows // 8)
+                ]
+                left = jnp.concatenate(parts, 0).astype(jnp.bfloat16)
+                lefts.append(jnp.concatenate([left, blank] if i % 2 == 0 else [blank, left], 1))
+            ones = []
+            for i in range(2):
+                high = jnp.where(sub < 4, highs[i], highs[i + 2])
+                mine = (jnp.bitwise_and(sub, 2) == 2 * i) & (high == jnp.bitwise_and(sub, 1))
+                ones.append(jnp.where(mine, 1.0, 0.0))
+            wleft = jnp.concatenate([jnp.concatenate(ones, 1), jnp.zeros((8, 2 * LANES), jnp.float32)], 0)
+            right = jnp.concatenate([jnp.concatenate(hots[:2], 1), jnp.concatenate(hots[2:], 1)], 0)
+            pltpu.matmul_push_rhs(right, k // 2, k % 2, transpose=True)
+            for i in range(PUSH):
+                pltpu.matmul_acc_lhs(sums[PUSH * k + i], lefts[i], load_staged_rhs=k // 2 if i == 0 else None)
+            pltpu.matmul_acc_lhs(wsums[k], wleft.astype(jnp.bfloat16))
+
+        def take(first, k):
+            for i in range(PUSH):
+                total = pltpu.matmul_pop(sums[PUSH * k + i])
+                grid_ref[tile_ref[first + PUSH * k + i]] += total[:, :LANES] if i < 2 else total[:, LANES:]
+            total = pltpu.matmul_pop(wsums[k])
+            for i in range(PUSH):
+                own = total[:8, :LANES] if i < 2 else total[:8, LANES:]
+                wgrid_ref[tile_ref[first + PUSH * k + i]] += jnp.where(jnp.right_shift(sub, 1) == i, own, 0.0)
+
+        def body(index, _):
+            first = pl.multiple_of(index * BATCH, BATCH)
+            data, weights = load(first)
+            for k in range(BATCH // PUSH):
+                take(first - BATCH, k)
+                feed(first, k, data, weights)
+            return 0
+
+        vis_copy(0).wait()
+        data, weights = load(0)
+        for k in range(BATCH // PUSH):
+            feed(0, k, data, weights)
+        for n in range(len(cuts)):
+            if n > 0:
+                vis_copy(n).wait()
+            low, high = max(1, starts[n] // BATCH), (starts[n] + cuts[n]) // BATCH
+            lax.fori_loop(low, high, body, 0, unroll=next((u for u in (8, 4, 3, 2) if (high - low) % u == 0 and high - low > u), 1))
+        for k in range(BATCH // PUSH):
+            take(groups - BATCH, k)
+
+    def space(unit, depth):
+        return pltpu.ACC(unit)((depth, 2 * LANES), jnp.float32)
+
+    pl.run_scoped(
+        inner,
+        *[space(k % 2, HALVES * rows) for k in range(BATCH // PUSH) for i in range(PUSH)],
+        *[space(k % 2, 16) for k in range(BATCH // PUSH)],
+    )
 
 
 def gridding(data, weight, tiles, offset, live, n_tile):
     rows, groups, slots = data.shape
-    block = math.gcd(groups, 64)
+    hbm = pl.BlockSpec(memory_space=pltpu.HBM)
+    vmem = pl.BlockSpec(memory_space=pltpu.VMEM)
     return pl.pallas_call(
         grid_kernel,
-        grid_spec=pltpu.PrefetchScalarGridSpec(
-            num_scalar_prefetch=2,
-            grid=(groups // block,),
-            in_specs=[
-                pl.BlockSpec((rows, block, slots), lambda i, *_: (0, i, 0)),
-                pl.BlockSpec((block, slots), lambda i, *_: (i, 0)),
-                pl.BlockSpec((block, slots), lambda i, *_: (i, 0)),
-            ],
-            out_specs=[
-                pl.BlockSpec((n_tile, HALVES * rows, LANES), lambda i, *_: (0, 0, 0), pipeline_mode=pl.Buffered(1)),
-                pl.BlockSpec((n_tile, 8, LANES), lambda i, *_: (0, 0, 0), pipeline_mode=pl.Buffered(1)),
-            ],
-        ),
+        in_specs=[hbm] * 5,
+        out_specs=[vmem, vmem],
         out_shape=[
             jax.ShapeDtypeStruct((n_tile, HALVES * rows, LANES), jnp.float32),
             jax.ShapeDtypeStruct((n_tile, 8, LANES), jnp.float32),
         ],
-        compiler_params=pltpu.CompilerParams(vmem_limit_bytes=20 << 20),
+        scratch_shapes=[
+            pltpu.SMEM(live.shape, jnp.int32),
+            pltpu.SMEM(tiles.shape, jnp.int32),
+            pltpu.VMEM(data.shape, data.dtype),
+            pltpu.VMEM(weight.shape, weight.dtype),
+            pltpu.VMEM(offset.shape, jnp.int32),
+            pltpu.SemaphoreType.DMA((len(chunks_of(groups)),)),
+            pltpu.SemaphoreType.DMA((4,)),
+        ],
+        compiler_params=pltpu.CompilerParams(vmem_limit_bytes=24 << 20),
         cost_estimate=pl.CostEstimate(flops=2 * groups * rows * slots * TILE, bytes_accessed=data.size * 2, transcendentals=0),
         name="gridding",
-    )(tiles, live, data, weight, offset)
+    )(*[in_hbm(x) for x in (live, tiles, data, weight, offset)])
 
 
 def dot3(left, right):
@@ -128,7 +210,7 @@
 
 def exchange_kernel(
     n_time, n_chan, per, grid_ref, wgrid_ref, delay_hbm, spread_hbm, out_ref,
-    ring, mine, gathered, wparts, delay, spread,
+    ring, mine, gathered, wparts, delay, spread, scale,
     ring_send, ring_recv, plane_send, plane_recv, w_send, w_recv, table_sem,
 ):
     me_t = lax.axis_index("tm")
@@ -155,15 +237,20 @@
         pl.semaphore_signal(barrier, inc=1, device_id={"chan": lax.rem(me_c + k, n_chan)}, device_id_type=MESH)
         return 0
 
-    lax.fori_loop(1, n_time, greet_t, 0)
+    greet_t(1, 0)
+    greet_t(n_time - 1, 0)
+    lax.fori_loop(2, n_time - 1, greet_t, 0)
     lax.fori_loop(1, n_chan, greet_c, 0)
     pl.semaphore_wait(barrier, n_time - 1 + n_chan - 1)
 
+    def piece_of(slot):
+        return lax.rem(slot + turn + 1, pieces)
+
     def span(slot):
-        return pl.ds(lax.rem(slot + turn, pieces) * per, per)
+        return pl.ds(piece_of(slot) * per, per)
 
     def grid_span(chunk, slot):
-        return pl.ds(chunk * n_chan + lax.rem(slot + turn, pieces) * per, per)
+        return pl.ds(chunk * n_chan + piece_of(slot) * per, per)
 
     def chunk_of(way, step):
         away = reach - step
@@ -229,13 +316,28 @@
             device_id_type=MESH,
         )
 
+    def w_wait(k, _):
+        w_copy(k).wait_recv()
+        return 0
+
+    lax.fori_loop(1, n_time, w_wait, 0)
+    wsum = wgrid_ref[me_t * n_chan + me_c]
+    for k in range(1, n_time):
+        wsum = wsum + wparts[k]
+    for copy in tables:
+        copy.wait()
+    halves = [sum(wsum[HALVES * i + a:HALVES * i + a + 1] for i in range(PUSH)) for a in range(HALVES)]
+    wcells = jnp.concatenate([jnp.broadcast_to(half, (8, LANES)) for half in halves], 1)
+    spread_pair = (spread[0], spread[1])
+    scale[...] = jnp.broadcast_to(1.0 / jnp.maximum(dot3(pair(wcells), spread_pair), 1.0), scale.shape)
+
     def finish(slot, _):
         for way in range(2):
             ring_copy(way, reach - 1, slot, True).wait_recv()
         where = span(slot)
         mine[where] = grid_ref[grid_span(me_t, slot)] + ring[0, reach - 1, where] + ring[1, reach - 1, where]
         for q in range(per):
-            other = lax.rem(slot + turn, pieces) * per + q
+            other = piece_of(slot) * per + q
 
             @pl.when(other != me_c)
             def _():
@@ -246,40 +348,38 @@
                 gathered[me_c] = mine[me_c]
         return 0
 
-    lax.fori_loop(0, pieces, finish, 0)
-
-    def w_wait(k, _):
-        w_copy(k).wait_recv()
-        return 0
-
-    lax.fori_loop(1, n_time, w_wait, 0)
-    wsum = wgrid_ref[me_t * n_chan + me_c]
-    for k in range(1, n_time):
-        wsum = wsum + wparts[k]
-    for copy in tables:
-        copy.wait()
-    wcells = jnp.concatenate([jnp.broadcast_to(wsum[a:a + 1], (8, LANES)) for a in range(HALVES)], 1)
-    spread_pair = (spread[0], spread[1])
-    scale = 1.0 / jnp.maximum(dot3(pair(wcells), spread_pair)[0:1], 1.0)
-
-    def plane_wait(k, _):
-        other = lax.rem(me_c + k, n_chan)
-        pltpu.make_async_remote_copy(
-            src_ref=mine.at[other],
-            dst_ref=gathered.at[other],
-            send_sem=plane_send.at[other],
-            recv_sem=plane_recv.at[other],
-            device_id={"chan": other},
-            device_id_type=MESH,
-        ).wait_recv()
-        return 0
-
-    lax.fori_loop(1, n_chan, plane_wait, 0)
-    cells = jnp.concatenate(
-        [gathered[:, a * rows:(a + 1) * rows, :].reshape(n_chan * rows, LANES) for a in range(HALVES)], 1
-    )
-    normal = pair(dot3(pair(cells), spread_pair) * scale)
-    out_ref[...] = dot3((delay[0], delay[1]), normal)
+    def absorb(slot, first):
+        block = lax.rem(turn + pieces - slot - 1 + pieces, pieces)
+        for q in range(per):
+            other = block * per + q
+
+            @pl.when(other != me_c)
+            def _():
+                pltpu.make_async_remote_copy(
+                    src_ref=mine.at[other],
+                    dst_ref=gathered.at[other],
+                    send_sem=plane_send.at[other],
+                    recv_sem=plane_recv.at[other],
+                    device_id={"chan": other},
+                    device_id_type=MESH,
+                ).wait_recv()
+
+        some = gathered[pl.ds(block * per, per)]
+        cells = jnp.concatenate([some[:, a * rows:(a + 1) * rows, :].reshape(per * rows, LANES) for a in range(HALVES)], 1)
+        normal = pair(dot3(pair(cells), spread_pair) * scale[0:1])
+        part = dot3((delay[0, block], delay[1, block]), normal)
+        out_ref[...] = part if first else out_ref[...] + part
+
+    def both(slot, _):
+        finish(slot, 0)
+        absorb(slot - 1, False)
+        return 0
+
+    finish(0, 0)
+    finish(1, 0)
+    absorb(0, True)
+    lax.fori_loop(2, pieces, both, 0)
+    absorb(pieces - 1, False)
 
     def drain_ring(way, step, low, high):
         lax.fori_loop(low, high, lambda slot, _: (ring_copy(way, step, slot, True).wait_send(), 0)[1], 0)
@@ -300,7 +400,8 @@
     per = max(1, n_chan // 8)
     pieces = n_chan // per
     reach = n_time // 2
-    delay = jnp.asarray(split_bf16(delay_table(total // 2)))
+    table = split_bf16(delay_table(total // 2)).reshape(2, total, pieces, per * rows)
+    delay = jnp.asarray(np.ascontiguousarray(table.transpose(0, 2, 1, 3)))
     spread = jnp.asarray(split_bf16(spread_table()))
     vmem = pl.BlockSpec(memory_space=pltpu.VMEM)
     hbm = pl.BlockSpec(memory_space=pl.ANY)
@@ -316,6 +417,7 @@
             pltpu.VMEM((n_time, 8, LANES), jnp.float32),
             pltpu.VMEM(delay.shape, jnp.bfloat16),
             pltpu.VMEM(spread.shape, jnp.bfloat16),
+            pltpu.VMEM((8, TILE), jnp.float32),
             pltpu.SemaphoreType.DMA((2, reach, pieces)),
             pltpu.SemaphoreType.DMA((2, reach, pieces)),
             pltpu.SemaphoreType.DMA((n_chan,)),
@@ -326,7 +428,7 @@
         ],
         compiler_params=pltpu.CompilerParams(collective_id=0, has_side_effects=True, vmem_limit_bytes=40 << 20),
         name="exchange",
-    )(grid, wgrid, delay, spread)
+    )(grid, wgrid, in_hbm(delay), in_hbm(spread))
 
 
 def local(visibilities, vis_weight, tile_index, tile_offset, live_count):
@@ -334,7 +436,7 @@
     n_chan = lax.axis_size("chan")
     n_time = lax.axis_size("tm")
     data = visibilities.reshape(channels * parts, groups, slots)
-    grid, wgrid = gridding(data, vis_weight, tile_index, tile_offset, live_count.reshape(groups), n_chan * n_time)
+    grid, wgrid = gridding(data, vis_weight, tile_index, tile_offset, live_count, n_chan * n_time)
     result = exchange(grid, wgrid, n_time, n_chan)
     return result.reshape(2, channels * n_chan, TILE)
 

time: 109 us -> 97.5 us (0.89)
  Pallas kernels: 102 us -> 96.5 us
  local copies, waits for them, and re-layouts: 5.83 us -> 0.88 us
    pallas_call x1, Pallas kernels: 20.1 us -> 10.7 us  [gridding(): pl.pallas_call(grid_kernel, in_specs=[hbm] * 5, out_specs=[vmem, vmem], o...]
    unnamed x13 -> x1, local copies, waits for them, and re-layouts: 5.83 us -> 0.88 us
    pallas_call x1, Pallas kernels: 82.2 us -> 85.7 us  [exchange(): pl.pallas_call(functools.partial(exchange_kernel, n_time, n_chan, per), i...]
where the time goes in v1:
time: 97.5 us; the launch traced here: 97.4 us
  Pallas kernels  96.5 us (99%)
    pallas_call x1, Pallas kernels, exchange(): pl.pallas_call(functools.partial(exchange_kernel, n_time, n_chan, per), i...  85.7 us
    pallas_call x1, Pallas kernels, gridding(): pl.pallas_call(grid_kernel, in_specs=[hbm] * 5, out_specs=[vmem, vmem], o...  10.7 us

profile of v1, /device:TPU:1, one launch (start us, length us, event | category | flops | bytes accessed | tf_op | source)
XLA Modules:
  0.0 97.4 jit_solution(14344600463263133783)
XLA Ops:
  0.0 10.7 %gridding.1 = (f32[256,48,128]{2,1,0:T(8,128)S(1)}, f32[256,8,128]{2,1,0:T(8,128)S(1)}) custom-call(s32[1,768]{1,0:T(1,128)} %live_hbm.1, s32[768]{0:T(1024)} %tile_hbm.1, bf16[24,768,128]{2,1,0:T(8,128)(2,1)} %bitcast.3, bf16[768,128]{1,0:T(8,128)(2,1)} %weight_hbm.1, s32[768,128]{1,0:T(8,128)} %offset_hbm.1), custom_call_target="tpu_custom_call" | custom-call | flops 1207959552 | bytes 4718592 | tf_op jit(solution)/shard_map/gridding/pallas_call | solution.py:178
  10.8 85.7 %exchange.1 = f32[768,256]{1,0:T(8,128)S(1)} custom-call(f32[256,48,128]{2,1,0:T(8,128)S(1)} %get-tuple-element.7.grid_ref, f32[256,8,128]{2,1,0:T(8,128)S(1)} %get-tuple-element.8.wgrid_ref, bf16[2,8,768,96]{3,2,1,0:T(8,128)(2,1)} %constant.4.clone.delay_hbm, bf16[2,256,256]{2,1,0:T(8,128)(2,1)} %constant.5.clone.spread_hbm), custom_call_target="tpu_custom_call" | custom-call | tf_op jit(solution)/shard_map/exchange/pallas_call | solution.py:408
  96.5 0.9 copy.9

commit v2 on v1

--- a/solution.py
+++ b/solution.py
@@ -210,13 +210,15 @@
 
 def exchange_kernel(
     n_time, n_chan, per, grid_ref, wgrid_ref, delay_hbm, spread_hbm, out_ref,
-    ring, mine, gathered, wparts, delay, spread, scale,
+    ring, mine, gathered, wown, wparts, delay, spread, scale,
     ring_send, ring_recv, plane_send, plane_recv, w_send, w_recv, table_sem,
 ):
     me_t = lax.axis_index("tm")
     me_c = lax.axis_index("chan")
     pieces = n_chan // per
+    wide = pieces // 2
     reach = n_time // 2
+    last = reach - 1
     rows2 = grid_ref.shape[1]
     rows = rows2 // HALVES
     turn = me_c // per
@@ -241,15 +243,30 @@
     greet_t(n_time - 1, 0)
     lax.fori_loop(2, n_time - 1, greet_t, 0)
     lax.fori_loop(1, n_chan, greet_c, 0)
+
+    for t in range(n_time):
+        part = wgrid_ref[t * n_chan + me_c]
+        total = part[0:HALVES]
+        for i in range(1, PUSH):
+            total = total + part[HALVES * i:HALVES * (i + 1)]
+        wown[t, 0:HALVES] = total
+
     pl.semaphore_wait(barrier, n_time - 1 + n_chan - 1)
 
+    def pair_of(slot):
+        return lax.rem(slot + turn // 2 + 1, wide)
+
     def piece_of(slot):
-        return lax.rem(slot + turn + 1, pieces)
-
-    def span(slot):
+        return 2 * pair_of(slot // 2) + lax.rem(slot + turn + 1, 2)
+
+    def span(step, slot):
+        if step < last:
+            return pl.ds(pair_of(slot) * (2 * per), 2 * per)
         return pl.ds(piece_of(slot) * per, per)
 
-    def grid_span(chunk, slot):
+    def grid_span(chunk, step, slot):
+        if step < last:
+            return pl.ds(chunk * n_chan + pair_of(slot) * (2 * per), 2 * per)
         return pl.ds(chunk * n_chan + piece_of(slot) * per, per)
 
     def chunk_of(way, step):
@@ -257,17 +274,18 @@
         return lax.rem(me_t + (away if way == 0 else n_time - away), n_time)
 
     def ring_copy(way, step, slot, raw):
-        source = grid_ref.at[grid_span(chunk_of(way, step), slot)] if raw else ring.at[way, step - 1, span(slot)]
+        where = span(step, slot)
+        source = grid_ref.at[grid_span(chunk_of(way, step), step, slot)] if raw else ring.at[way, step - 1, where]
         return pltpu.make_async_remote_copy(
             src_ref=source,
-            dst_ref=ring.at[way, step, span(slot)],
+            dst_ref=ring.at[way, step, where],
             send_sem=ring_send.at[way, step, slot],
             recv_sem=ring_recv.at[way, step, slot],
             device_id={"tm": neighbour[way]},
             device_id_type=MESH,
         )
 
-    half = pieces // 2
+    half = wide // 2
 
     def open_ring(slot, _):
         ring_copy(0, 0, slot, True).start()
@@ -279,8 +297,8 @@
     def w_copy(k):
         other = lax.rem(me_t + k, n_time)
         return pltpu.make_async_remote_copy(
-            src_ref=wgrid_ref.at[other * n_chan + me_c],
-            dst_ref=wparts.at[k],
+            src_ref=wown.at[other, pl.ds(0, HALVES)],
+            dst_ref=wparts.at[k, pl.ds(0, HALVES)],
             send_sem=w_send.at[k],
             recv_sem=w_recv.at[k],
             device_id={"tm": other},
@@ -292,19 +310,22 @@
     def hop(step, fresh):
         def body(slot, _):
             for way in range(2):
-                if fresh[way]:
-                    ring_copy(way, step, slot, True).start()
-                else:
+                if not fresh[way]:
                     ring_copy(way, step - 1, slot, True).wait_recv()
-                    ring[way, step - 1, span(slot)] += grid_ref[grid_span(chunk_of(way, step), slot)]
-                    ring_copy(way, step, slot, False).start()
+                    ring[way, step - 1, span(step - 1, slot)] += grid_ref[grid_span(chunk_of(way, step), step - 1, slot)]
+                if step < last:
+                    ring_copy(way, step, slot, fresh[way]).start()
+            if step == last:
+                for q in range(2):
+                    for way in range(2):
+                        ring_copy(way, step, 2 * slot + q, fresh[way]).start()
             return 0
         return body
 
     lax.fori_loop(0, half, hop(1, (False, True)), 0)
-    lax.fori_loop(half, pieces, hop(1, (True, False)), 0)
+    lax.fori_loop(half, wide, hop(1, (True, False)), 0)
     for step in range(2, reach):
-        lax.fori_loop(0, pieces, hop(step, (False, False)), 0)
+        lax.fori_loop(0, wide, hop(step, (False, False)), 0)
 
     def plane_copy(other):
         return pltpu.make_async_remote_copy(
@@ -316,26 +337,21 @@
             device_id_type=MESH,
         )
 
-    def w_wait(k, _):
-        w_copy(k).wait_recv()
-        return 0
-
-    lax.fori_loop(1, n_time, w_wait, 0)
-    wsum = wgrid_ref[me_t * n_chan + me_c]
+    lax.fori_loop(1, n_time, lambda k, _: (w_copy(k).wait_recv(), 0)[1], 0)
+    wsum = wown[me_t, 0:HALVES]
     for k in range(1, n_time):
-        wsum = wsum + wparts[k]
+        wsum = wsum + wparts[k, 0:HALVES]
     for copy in tables:
         copy.wait()
-    halves = [sum(wsum[HALVES * i + a:HALVES * i + a + 1] for i in range(PUSH)) for a in range(HALVES)]
-    wcells = jnp.concatenate([jnp.broadcast_to(half, (8, LANES)) for half in halves], 1)
+    wcells = jnp.concatenate([jnp.broadcast_to(wsum[a:a + 1], (8, LANES)) for a in range(HALVES)], 1)
     spread_pair = (spread[0], spread[1])
     scale[...] = jnp.broadcast_to(1.0 / jnp.maximum(dot3(pair(wcells), spread_pair), 1.0), scale.shape)
 
     def finish(slot, _):
         for way in range(2):
-            ring_copy(way, reach - 1, slot, True).wait_recv()
-        where = span(slot)
-        mine[where] = grid_ref[grid_span(me_t, slot)] + ring[0, reach - 1, where] + ring[1, reach - 1, where]
+            ring_copy(way, last, slot, True).wait_recv()
+        where = span(last, slot)
+        mine[where] = grid_ref[grid_span(me_t, last, slot)] + ring[0, last, where] + ring[1, last, where]
         for q in range(per):
             other = piece_of(slot) * per + q
 
@@ -349,7 +365,7 @@
         return 0
 
     def absorb(slot, first):
-        block = lax.rem(turn + pieces - slot - 1 + pieces, pieces)
+        block = 2 * lax.rem(turn // 2 + pieces - slot // 2 - 1, wide) + lax.rem(turn + pieces - slot - 1, 2)
         for q in range(per):
             other = block * per + q
 
@@ -370,26 +386,28 @@
         part = dot3((delay[0, block], delay[1, block]), normal)
         out_ref[...] = part if first else out_ref[...] + part
 
+    lag = min(3, pieces - 1)
+
     def both(slot, _):
         finish(slot, 0)
-        absorb(slot - 1, False)
+        absorb(slot - lag, False)
         return 0
 
-    finish(0, 0)
-    finish(1, 0)
+    lax.fori_loop(0, lag + 1, finish, 0)
     absorb(0, True)
-    lax.fori_loop(2, pieces, both, 0)
-    absorb(pieces - 1, False)
+    lax.fori_loop(lag + 1, pieces, both, 0)
 
     def drain_ring(way, step, low, high):
         lax.fori_loop(low, high, lambda slot, _: (ring_copy(way, step, slot, True).wait_send(), 0)[1], 0)
 
     drain_ring(0, 0, 0, half)
-    drain_ring(1, 0, half, pieces)
+    drain_ring(1, 0, half, wide)
     for step in range(1, reach):
         for way in range(2):
-            drain_ring(way, step, 0, pieces)
+            drain_ring(way, step, 0, wide if step < last else pieces)
     lax.fori_loop(1, n_time, lambda k, _: (w_copy(k).wait_send(), 0)[1], 0)
+
+    lax.fori_loop(pieces - lag, pieces, lambda k, _: (absorb(k, False), 0)[1], 0)
     lax.fori_loop(1, n_chan, lambda k, _: (plane_copy(lax.rem(me_c + k, n_chan)).wait_send(), 0)[1], 0)
 
 
@@ -415,6 +433,7 @@
             pltpu.VMEM((n_chan, rows2, LANES), jnp.float32),
             pltpu.VMEM((n_chan, rows2, LANES), jnp.float32),
             pltpu.VMEM((n_time, 8, LANES), jnp.float32),
+            pltpu.VMEM((n_time, 8, LANES), jnp.float32),
             pltpu.VMEM(delay.shape, jnp.bfloat16),
             pltpu.VMEM(spread.shape, jnp.bfloat16),
             pltpu.VMEM((8, TILE), jnp.float32),

time: 97.5 us -> 90.6 us (0.929)
  Pallas kernels: 96.5 us -> 89.7 us
    pallas_call x1, Pallas kernels: 85.7 us -> 78.9 us  [exchange(): pl.pallas_call(functools.partial(exchange_kernel, n_time, n_chan, per), i...]
where the time goes in v2:
time: 90.6 us
  Pallas kernels  89.7 us (99%)
    pallas_call x1, Pallas kernels, exchange(): pl.pallas_call(functools.partial(exchange_kernel, n_time, n_chan, per), i...  78.9 us
    pallas_call x1, Pallas kernels, gridding(): pl.pallas_call(grid_kernel, in_specs=[hbm] * 5, out_specs=[vmem, vmem], o...  10.8 us

profile of v2, /device:TPU:1, one launch (start us, length us, event | category | flops | bytes accessed | tf_op | source)
XLA Modules:
  0.0 90.6 jit_solution(11555167828272744504)
XLA Ops:
  0.0 10.8 %gridding.1 = (f32[256,48,128]{2,1,0:T(8,128)S(1)}, f32[256,8,128]{2,1,0:T(8,128)S(1)}) custom-call(s32[1,768]{1,0:T(1,128)} %live_hbm.1, s32[768]{0:T(1024)} %tile_hbm.1, bf16[24,768,128]{2,1,0:T(8,128)(2,1)} %bitcast.3, bf16[768,128]{1,0:T(8,128)(2,1)} %weight_hbm.1, s32[768,128]{1,0:T(8,128)} %offset_hbm.1), custom_call_target="tpu_custom_call" | custom-call | flops 1207959552 | bytes 4718592 | tf_op jit(solution)/shard_map/gridding/pallas_call | solution.py:178
  10.8 78.9 %exchange.1 = f32[768,256]{1,0:T(8,128)S(1)} custom-call(f32[256,48,128]{2,1,0:T(8,128)S(1)} %get-tuple-element.7.grid_ref, f32[256,8,128]{2,1,0:T(8,128)S(1)} %get-tuple-element.8.wgrid_ref, bf16[2,8,768,96]{3,2,1,0:T(8,128)(2,1)} %constant.4.clone.delay_hbm, bf16[2,256,256]{2,1,0:T(8,128)(2,1)} %constant.5.clone.spread_hbm), custom_call_target="tpu_custom_call" | custom-call | tf_op jit(solution)/shard_map/exchange/pallas_call | solution.py:426
  89.7 0.9 copy.9

commit v3 on v2

--- a/solution.py
+++ b/solution.py
@@ -126,8 +126,11 @@
                 mine = (jnp.bitwise_and(sub, 2) == 2 * i) & (high == jnp.bitwise_and(sub, 1))
                 ones.append(jnp.where(mine, 1.0, 0.0))
             wleft = jnp.concatenate([jnp.concatenate(ones, 1), jnp.zeros((8, 2 * LANES), jnp.float32)], 0)
+            turned = k >= BATCH // PUSH // 2
+            if turned:
+                hots = [hots[i].T for i in (0, 2, 1, 3)]
             right = jnp.concatenate([jnp.concatenate(hots[:2], 1), jnp.concatenate(hots[2:], 1)], 0)
-            pltpu.matmul_push_rhs(right, k // 2, k % 2, transpose=True)
+            pltpu.matmul_push_rhs(right, k // 2, k % 2, transpose=not turned)
             for i in range(PUSH):
                 pltpu.matmul_acc_lhs(sums[PUSH * k + i], lefts[i], load_staged_rhs=k // 2 if i == 0 else None)
             pltpu.matmul_acc_lhs(wsums[k], wleft.astype(jnp.bfloat16))
@@ -219,6 +222,7 @@
     wide = pieces // 2
     reach = n_time // 2
     last = reach - 1
+    fine = 2 if per % 2 == 0 else 1
     rows2 = grid_ref.shape[1]
     rows = rows2 // HALVES
     turn = me_c // per
@@ -244,13 +248,6 @@
     lax.fori_loop(2, n_time - 1, greet_t, 0)
     lax.fori_loop(1, n_chan, greet_c, 0)
 
-    for t in range(n_time):
-        part = wgrid_ref[t * n_chan + me_c]
-        total = part[0:HALVES]
-        for i in range(1, PUSH):
-            total = total + part[HALVES * i:HALVES * (i + 1)]
-        wown[t, 0:HALVES] = total
-
     pl.semaphore_wait(barrier, n_time - 1 + n_chan - 1)
 
     def pair_of(slot):
@@ -262,12 +259,12 @@
     def span(step, slot):
         if step < last:
             return pl.ds(pair_of(slot) * (2 * per), 2 * per)
-        return pl.ds(piece_of(slot) * per, per)
+        return pl.ds(piece_of(slot // fine) * per + lax.rem(slot, fine) * (per // fine), per // fine)
 
     def grid_span(chunk, step, slot):
         if step < last:
             return pl.ds(chunk * n_chan + pair_of(slot) * (2 * per), 2 * per)
-        return pl.ds(chunk * n_chan + piece_of(slot) * per, per)
+        return pl.ds(chunk * n_chan + piece_of(slot // fine) * per + lax.rem(slot, fine) * (per // fine), per // fine)
 
     def chunk_of(way, step):
         away = reach - step
@@ -294,6 +291,13 @@
 
     lax.fori_loop(0, half, open_ring, 0)
 
+    for t in range(n_time):
+        part = wgrid_ref[t * n_chan + me_c]
+        total = part[0:HALVES]
+        for i in range(1, PUSH):
+            total = total + part[HALVES * i:HALVES * (i + 1)]
+        wown[t, 0:HALVES] = total
+
     def w_copy(k):
         other = lax.rem(me_t + k, n_time)
         return pltpu.make_async_remote_copy(
@@ -316,9 +320,9 @@
                 if step < last:
                     ring_copy(way, step, slot, fresh[way]).start()
             if step == last:
-                for q in range(2):
+                for q in range(2 * fine):
                     for way in range(2):
-                        ring_copy(way, step, 2 * slot + q, fresh[way]).start()
+                        ring_copy(way, step, 2 * fine * slot + q, fresh[way]).start()
             return 0
         return body
 
@@ -352,8 +356,8 @@
             ring_copy(way, last, slot, True).wait_recv()
         where = span(last, slot)
         mine[where] = grid_ref[grid_span(me_t, last, slot)] + ring[0, last, where] + ring[1, last, where]
-        for q in range(per):
-            other = piece_of(slot) * per + q
+        for q in range(per // fine):
+            other = piece_of(slot // fine) * per + lax.rem(slot, fine) * (per // fine) + q
 
             @pl.when(other != me_c)
             def _():
@@ -382,18 +386,20 @@
 
         some = gathered[pl.ds(block * per, per)]
         cells = jnp.concatenate([some[:, a * rows:(a + 1) * rows, :].reshape(per * rows, LANES) for a in range(HALVES)], 1)
-        normal = pair(dot3(pair(cells), spread_pair) * scale[0:1])
-        part = dot3((delay[0, block], delay[1, block]), normal)
+        normal = dot3(pair(cells), spread_pair) * scale[0:1]
+        high, low = pair(normal)
+        part = jnp.dot(delay[block], jnp.concatenate([high, high, low], 0), preferred_element_type=jnp.float32)
         out_ref[...] = part if first else out_ref[...] + part
 
     lag = min(3, pieces - 1)
 
     def both(slot, _):
-        finish(slot, 0)
+        for f in range(fine):
+            finish(slot * fine + f, 0)
         absorb(slot - lag, False)
         return 0
 
-    lax.fori_loop(0, lag + 1, finish, 0)
+    lax.fori_loop(0, (lag + 1) * fine, finish, 0)
     absorb(0, True)
     lax.fori_loop(lag + 1, pieces, both, 0)
 
@@ -404,7 +410,7 @@
     drain_ring(1, 0, half, wide)
     for step in range(1, reach):
         for way in range(2):
-            drain_ring(way, step, 0, wide if step < last else pieces)
+            drain_ring(way, step, 0, wide if step < last else pieces * fine)
     lax.fori_loop(1, n_time, lambda k, _: (w_copy(k).wait_send(), 0)[1], 0)
 
     lax.fori_loop(pieces - lag, pieces, lambda k, _: (absorb(k, False), 0)[1], 0)
@@ -419,7 +425,7 @@
     pieces = n_chan // per
     reach = n_time // 2
     table = split_bf16(delay_table(total // 2)).reshape(2, total, pieces, per * rows)
-    delay = jnp.asarray(np.ascontiguousarray(table.transpose(0, 2, 1, 3)))
+    delay = jnp.asarray(np.concatenate([table[0], table[1], table[0]], -1).transpose(1, 0, 2))
     spread = jnp.asarray(split_bf16(spread_table()))
     vmem = pl.BlockSpec(memory_space=pltpu.VMEM)
     hbm = pl.BlockSpec(memory_space=pl.ANY)
@@ -437,8 +443,8 @@
             pltpu.VMEM(delay.shape, jnp.bfloat16),
             pltpu.VMEM(spread.shape, jnp.bfloat16),
             pltpu.VMEM((8, TILE), jnp.float32),
-            pltpu.SemaphoreType.DMA((2, reach, pieces)),
-            pltpu.SemaphoreType.DMA((2, reach, pieces)),
+            pltpu.SemaphoreType.DMA((2, reach, 2 * pieces)),
+            pltpu.SemaphoreType.DMA((2, reach, 2 * pieces)),
             pltpu.SemaphoreType.DMA((n_chan,)),
             pltpu.SemaphoreType.DMA((n_chan,)),
             pltpu.SemaphoreType.DMA((n_time,)),

time: 90.6 us -> 89.6 us (0.989)
  Pallas kernels: 89.7 us -> 88.6 us
    pallas_call x1, Pallas kernels: 10.8 us -> 9.46 us  [gridding(): pl.pallas_call(grid_kernel, in_specs=[hbm] * 5, out_specs=[vmem, vmem], o...]
where the time goes in v3:
time: 89.6 us; the launch traced here: 89.5 us
  Pallas kernels  88.6 us (99%)
    pallas_call x1, Pallas kernels, exchange(): pl.pallas_call(functools.partial(exchange_kernel, n_time, n_chan, per), i...  79.1 us
    pallas_call x1, Pallas kernels, gridding(): pl.pallas_call(grid_kernel, in_specs=[hbm] * 5, out_specs=[vmem, vmem], o...  9.46 us

profile of v3, /device:TPU:1, one launch (start us, length us, event | category | flops | bytes accessed | tf_op | source)
XLA Modules:
  0.0 89.5 jit_solution(1606910883958861622)
XLA Ops:
  0.0 9.5 %gridding.1 = (f32[256,48,128]{2,1,0:T(8,128)S(1)}, f32[256,8,128]{2,1,0:T(8,128)S(1)}) custom-call(s32[1,768]{1,0:T(1,128)} %live_hbm.1, s32[768]{0:T(1024)} %tile_hbm.1, bf16[24,768,128]{2,1,0:T(8,128)(2,1)} %bitcast.3, bf16[768,128]{1,0:T(8,128)(2,1)} %weight_hbm.1, s32[768,128]{1,0:T(8,128)} %offset_hbm.1), custom_call_target="tpu_custom_call" | custom-call | flops 1207959552 | bytes 4718592 | tf_op jit(solution)/shard_map/gridding/pallas_call | solution.py:181
  9.5 79.1 %exchange.1 = f32[768,256]{1,0:T(8,128)S(1)} custom-call(f32[256,48,128]{2,1,0:T(8,128)S(1)} %get-tuple-element.7.grid_ref, f32[256,8,128]{2,1,0:T(8,128)S(1)} %get-tuple-element.8.wgrid_ref, bf16[8,768,288]{2,1,0:T(8,128)(2,1)} %constant.4.clone.delay_hbm, bf16[2,256,256]{2,1,0:T(8,128)(2,1)} %constant.5.clone.spread_hbm), custom_call_target="tpu_custom_call" | custom-call | tf_op jit(solution)/shard_map/exchange/pallas_call | solution.py:432
  88.6 0.9 copy.9

commit v4 on v3

--- a/solution.py
+++ b/solution.py
@@ -250,8 +250,14 @@
 
     pl.semaphore_wait(barrier, n_time - 1 + n_chan - 1)
 
+    def away(slot):
+        if wide != 4:
+            return lax.rem(slot + 1, wide)
+        late = slot // 2
+        return (2 + slot) * (1 - late) + (3 - slot) * late
+
     def pair_of(slot):
-        return lax.rem(slot + turn // 2 + 1, wide)
+        return lax.rem(away(slot) + turn // 2, wide)
 
     def piece_of(slot):
         return 2 * pair_of(slot // 2) + lax.rem(slot + turn + 1, 2)
@@ -267,8 +273,8 @@
         return pl.ds(chunk * n_chan + piece_of(slot // fine) * per + lax.rem(slot, fine) * (per // fine), per // fine)
 
     def chunk_of(way, step):
-        away = reach - step
-        return lax.rem(me_t + (away if way == 0 else n_time - away), n_time)
+        hops = reach - step
+        return lax.rem(me_t + (hops if way == 0 else n_time - hops), n_time)
 
     def ring_copy(way, step, slot, raw):
         where = span(step, slot)
@@ -369,7 +375,7 @@
         return 0
 
     def absorb(slot, first):
-        block = 2 * lax.rem(turn // 2 + pieces - slot // 2 - 1, wide) + lax.rem(turn + pieces - slot - 1, 2)
+        block = 2 * lax.rem(turn // 2 + wide - away(slot // 2), wide) + lax.rem(turn + pieces - slot - 1, 2)
         for q in range(per):
             other = block * per + q
 
@@ -393,28 +399,35 @@
 
     lag = min(3, pieces - 1)
 
-    def both(slot, _):
+    def whole(slot):
         for f in range(fine):
             finish(slot * fine + f, 0)
+
+    def both(slot, _):
         absorb(slot - lag, False)
+        whole(slot)
         return 0
-
-    lax.fori_loop(0, (lag + 1) * fine, finish, 0)
-    absorb(0, True)
-    lax.fori_loop(lag + 1, pieces, both, 0)
 
     def drain_ring(way, step, low, high):
         lax.fori_loop(low, high, lambda slot, _: (ring_copy(way, step, slot, True).wait_send(), 0)[1], 0)
 
     drain_ring(0, 0, 0, half)
     drain_ring(1, 0, half, wide)
-    for step in range(1, reach):
+    for step in range(1, last):
         for way in range(2):
-            drain_ring(way, step, 0, wide if step < last else pieces * fine)
+            drain_ring(way, step, 0, wide)
     lax.fori_loop(1, n_time, lambda k, _: (w_copy(k).wait_send(), 0)[1], 0)
 
-    lax.fori_loop(pieces - lag, pieces, lambda k, _: (absorb(k, False), 0)[1], 0)
+    for slot in range(lag):
+        whole(slot)
+    absorb(0, True)
+    whole(lag)
+    lax.fori_loop(lag + 1, pieces, both, 0)
+    for way in range(2):
+        drain_ring(way, last, 0, pieces * fine)
+    lax.fori_loop(pieces - lag, pieces - 1, lambda k, _: (absorb(k, False), 0)[1], 0)
     lax.fori_loop(1, n_chan, lambda k, _: (plane_copy(lax.rem(me_c + k, n_chan)).wait_send(), 0)[1], 0)
+    absorb(pieces - 1, False)
 
 
 def exchange(grid, wgrid, n_time, n_chan):

time: 89.6 us -> 89.2 us (level)
  no operation moved by 1% of the time
where the time goes in v4:
time: 89.2 us; the launch traced here: 89.1 us
  Pallas kernels  88.2 us (99%)
    pallas_call x1, Pallas kernels, exchange(): pl.pallas_call(functools.partial(exchange_kernel, n_time, n_chan, per), i...  78.8 us
    pallas_call x1, Pallas kernels, gridding(): pl.pallas_call(grid_kernel, in_specs=[hbm] * 5, out_specs=[vmem, vmem], o...  9.44 us

profile of v4, /device:TPU:1, one launch (start us, length us, event | category | flops | bytes accessed | tf_op | source)
XLA Modules:
  0.0 89.1 jit_solution(17059452926937215679)
XLA Ops:
  0.0 9.4 %gridding.1 = (f32[256,48,128]{2,1,0:T(8,128)S(1)}, f32[256,8,128]{2,1,0:T(8,128)S(1)}) custom-call(s32[1,768]{1,0:T(1,128)} %live_hbm.1, s32[768]{0:T(1024)} %tile_hbm.1, bf16[24,768,128]{2,1,0:T(8,128)(2,1)} %bitcast.3, bf16[768,128]{1,0:T(8,128)(2,1)} %weight_hbm.1, s32[768,128]{1,0:T(8,128)} %offset_hbm.1), custom_call_target="tpu_custom_call" | custom-call | flops 1207959552 | bytes 4718592 | tf_op jit(solution)/shard_map/gridding/pallas_call | solution.py:181
  9.4 78.8 %exchange.1 = f32[768,256]{1,0:T(8,128)S(1)} custom-call(f32[256,48,128]{2,1,0:T(8,128)S(1)} %get-tuple-element.7.grid_ref, f32[256,8,128]{2,1,0:T(8,128)S(1)} %get-tuple-element.8.wgrid_ref, bf16[8,768,288]{2,1,0:T(8,128)(2,1)} %constant.4.clone.delay_hbm, bf16[2,256,256]{2,1,0:T(8,128)(2,1)} %constant.5.clone.spread_hbm), custom_call_target="tpu_custom_call" | custom-call | tf_op jit(solution)/shard_map/exchange/pallas_call | solution.py:445
  88.2 0.9 copy.9

commit v5 on v4

--- a/solution.py
+++ b/solution.py
@@ -55,8 +55,7 @@
     cuts = [32, 96, 128]
     if groups < 2 * sum(cuts):
         return [groups]
-    rest = groups - sum(cuts)
-    return cuts + [rest // 2, rest - rest // 2]
+    return cuts + [groups - sum(cuts)]
 
 
 def grid_kernel(
@@ -160,7 +159,7 @@
             if n > 0:
                 vis_copy(n).wait()
             low, high = max(1, starts[n] // BATCH), (starts[n] + cuts[n]) // BATCH
-            lax.fori_loop(low, high, body, 0, unroll=next((u for u in (8, 4, 3, 2) if (high - low) % u == 0 and high - low > u), 1))
+            lax.fori_loop(low, high, body, 0, unroll=next((u for u in (16, 8, 4, 3, 2) if (high - low) % u == 0 and high - low > u), 1))
         for k in range(BATCH // PUSH):
             take(groups - BATCH, k)
 

time: 89.2 us -> 88.8 us (level)
  no operation moved by 1% of the time
where the time goes in v5:
time: 88.8 us; the launch traced here: 88.7 us
  Pallas kernels  87.8 us (99%)
    pallas_call x1, Pallas kernels, exchange(): pl.pallas_call(functools.partial(exchange_kernel, n_time, n_chan, per), i...  78.8 us
    pallas_call x1, Pallas kernels, gridding(): pl.pallas_call(grid_kernel, in_specs=[hbm] * 5, out_specs=[vmem, vmem], o...  9.03 us

profile of v5, /device:TPU:1, one launch (start us, length us, event | category | flops | bytes accessed | tf_op | source)
XLA Modules:
  0.0 88.7 jit_solution(4431215499686594816)
XLA Ops:
  0.0 9.0 %gridding.1 = (f32[256,48,128]{2,1,0:T(8,128)S(1)}, f32[256,8,128]{2,1,0:T(8,128)S(1)}) custom-call(s32[1,768]{1,0:T(1,128)} %live_hbm.1, s32[768]{0:T(1024)} %tile_hbm.1, bf16[24,768,128]{2,1,0:T(8,128)(2,1)} %bitcast.3, bf16[768,128]{1,0:T(8,128)(2,1)} %weight_hbm.1, s32[768,128]{1,0:T(8,128)} %offset_hbm.1), custom_call_target="tpu_custom_call" | custom-call | flops 1207959552 | bytes 4718592 | tf_op jit(solution)/shard_map/gridding/pallas_call | solution.py:180
  9.0 78.8 %exchange.1 = f32[768,256]{1,0:T(8,128)S(1)} custom-call(f32[256,48,128]{2,1,0:T(8,128)S(1)} %get-tuple-element.7.grid_ref, f32[256,8,128]{2,1,0:T(8,128)S(1)} %get-tuple-element.8.wgrid_ref, bf16[8,768,288]{2,1,0:T(8,128)(2,1)} %constant.4.clone.delay_hbm, bf16[2,256,256]{2,1,0:T(8,128)(2,1)} %constant.5.clone.spread_hbm), custom_call_target="tpu_custom_call" | custom-call | tf_op jit(solution)/shard_map/exchange/pallas_call | solution.py:444
  87.9 0.9 copy.9

commit v6 on v5

--- a/solution.py
+++ b/solution.py
@@ -70,13 +70,23 @@
         part = pl.ds(starts[n], cuts[n])
         return pltpu.make_async_copy(vis_hbm.at[:, part], vis_ref.at[:, part], vis_sem.at[n])
 
-    pairs = [(weight_hbm, weight_ref), (offset_hbm, offset_ref), (live_hbm, live_ref), (tile_hbm, tile_ref)]
+    head = sum(cuts[:2])
+    pairs = [(live_hbm, live_ref), (tile_hbm, tile_ref)]
+    later = []
+    for source, target in ((offset_hbm, offset_ref), (weight_hbm, weight_ref)):
+        pairs.append((source.at[pl.ds(0, head)], target.at[pl.ds(0, head)]))
+        if head < groups:
+            rest = pl.ds(head, groups - head)
+            later.append((source.at[rest], target.at[rest]))
     small = [pltpu.make_async_copy(a, b, small_sem.at[n]) for n, (a, b) in enumerate(pairs)]
-    vis_copy(0).start()
+    later = [pltpu.make_async_copy(a, b, small_sem.at[len(pairs) + n]) for n, (a, b) in enumerate(later)]
     for copy in small:
         copy.start()
-    for n in range(1, len(cuts)):
+    for n in range(len(cuts)):
         vis_copy(n).start()
+        if n == 1:
+            for copy in later:
+                copy.start()
 
     @pl.loop(0, grid_ref.shape[0] // 8)
     def _(i):
@@ -158,6 +168,9 @@
         for n in range(len(cuts)):
             if n > 0:
                 vis_copy(n).wait()
+            if n == 2:
+                for copy in later:
+                    copy.wait()
             low, high = max(1, starts[n] // BATCH), (starts[n] + cuts[n]) // BATCH
             lax.fori_loop(low, high, body, 0, unroll=next((u for u in (16, 8, 4, 3, 2) if (high - low) % u == 0 and high - low > u), 1))
         for k in range(BATCH // PUSH):
@@ -192,7 +205,7 @@
             pltpu.VMEM(weight.shape, weight.dtype),
             pltpu.VMEM(offset.shape, jnp.int32),
             pltpu.SemaphoreType.DMA((len(chunks_of(groups)),)),
-            pltpu.SemaphoreType.DMA((4,)),
+            pltpu.SemaphoreType.DMA((6,)),
         ],
         compiler_params=pltpu.CompilerParams(vmem_limit_bytes=24 << 20),
         cost_estimate=pl.CostEstimate(flops=2 * groups * rows * slots * TILE, bytes_accessed=data.size * 2, transcendentals=0),
@@ -227,25 +240,25 @@
     turn = me_c // per
     neighbour = (lax.rem(me_t + 1, n_time), lax.rem(me_t + n_time - 1, n_time))
 
+    barrier = pltpu.get_barrier_semaphore()
+
+    def greet_t(k, _):
+        pl.semaphore_signal(barrier, inc=1, device_id={"tm": lax.rem(me_t + k, n_time)}, device_id_type=MESH)
+        return 0
+
+    def greet_c(k, _):
+        pl.semaphore_signal(barrier, inc=1, device_id={"chan": lax.rem(me_c + k, n_chan)}, device_id_type=MESH)
+        return 0
+
+    greet_t(1, 0)
+    greet_t(n_time - 1, 0)
+    lax.fori_loop(2, n_time - 1, greet_t, 0)
+    lax.fori_loop(1, n_chan, greet_c, 0)
+
     tables = [pltpu.make_async_copy(delay_hbm, delay, table_sem.at[0]),
               pltpu.make_async_copy(spread_hbm, spread, table_sem.at[1])]
     for copy in tables:
         copy.start()
-
-    barrier = pltpu.get_barrier_semaphore()
-
-    def greet_t(k, _):
-        pl.semaphore_signal(barrier, inc=1, device_id={"tm": lax.rem(me_t + k, n_time)}, device_id_type=MESH)
-        return 0
-
-    def greet_c(k, _):
-        pl.semaphore_signal(barrier, inc=1, device_id={"chan": lax.rem(me_c + k, n_chan)}, device_id_type=MESH)
-        return 0
-
-    greet_t(1, 0)
-    greet_t(n_time - 1, 0)
-    lax.fori_loop(2, n_time - 1, greet_t, 0)
-    lax.fori_loop(1, n_chan, greet_c, 0)
 
     pl.semaphore_wait(barrier, n_time - 1 + n_chan - 1)
 

time: 88.8 us -> 88.5 us (level)
  no operation moved by 1% of the time
where the time goes in v6:
time: 88.5 us; the launch traced here: 88.4 us
  Pallas kernels  87.5 us (99%)
    pallas_call x1, Pallas kernels, exchange(): pl.pallas_call(functools.partial(exchange_kernel, n_time, n_chan, per), i...  78.8 us
    pallas_call x1, Pallas kernels, gridding(): pl.pallas_call(grid_kernel, in_specs=[hbm] * 5, out_specs=[vmem, vmem], o...  8.76 us

profile of v6, /device:TPU:1, one launch (start us, length us, event | category | flops | bytes accessed | tf_op | source)
XLA Modules:
  0.0 88.4 jit_solution(13788995450274953104)
XLA Ops:
  0.0 8.8 %gridding.1 = (f32[256,48,128]{2,1,0:T(8,128)S(1)}, f32[256,8,128]{2,1,0:T(8,128)S(1)}) custom-call(s32[1,768]{1,0:T(1,128)} %live_hbm.1, s32[768]{0:T(1024)} %tile_hbm.1, bf16[24,768,128]{2,1,0:T(8,128)(2,1)} %bitcast.3, bf16[768,128]{1,0:T(8,128)(2,1)} %weight_hbm.1, s32[768,128]{1,0:T(8,128)} %offset_hbm.1), custom_call_target="tpu_custom_call" | custom-call | flops 1207959552 | bytes 4718592 | tf_op jit(solution)/shard_map/gridding/pallas_call | solution.py:193
  8.8 78.8 %exchange.1 = f32[768,256]{1,0:T(8,128)S(1)} custom-call(f32[256,48,128]{2,1,0:T(8,128)S(1)} %get-tuple-element.7.grid_ref, f32[256,8,128]{2,1,0:T(8,128)S(1)} %get-tuple-element.8.wgrid_ref, bf16[8,768,288]{2,1,0:T(8,128)(2,1)} %constant.4.clone.delay_hbm, bf16[2,256,256]{2,1,0:T(8,128)(2,1)} %constant.5.clone.spread_hbm), custom_call_target="tpu_custom_call" | custom-call | tf_op jit(solution)/shard_map/exchange/pallas_call | solution.py:457
  87.6 0.9 copy.9
